TPU v7x, 512 devices: a whole 4x4x16 slice. The times are simulated.
512 devices in a mesh: row: 16 (over z), col: 8 (over x, core), rep: 4 (over y).
Axes of the slice: x: 4, y: 4, z: 16, core: 2. Of those that a mesh axis runs over, the one named last changes fastest.
Arguments:
- density: bfloat16 [6144, 6144], P('row', 'col'), as said below
- keep_square: int32 [48, 48], P('row', 'col'), may hold values 0 or 1
- keep_cube: int32 [48, 48], P('row', 'col'), may hold values 0 or 1
Outputs:
- purified: float32 [6144, 6144], P(('row', 'rep'), 'col')
Inputs may be any that keep to these rules, and one draw needn't show every extreme that they name: density is symmetric; its 128 x 128 diagonal blocks are always occupied, any other block may be zero or occupied at any distance from the diagonal.
All inputs are finite; a program needn't handle non-finite values. No bound on the sum of `keep_square` or of `keep_cube` on one device may be relied on, other than what follows from the above.
Results may differ from a plain program's by a relative error of at most 0.002.
Values may be sent and summed in bfloat16 or wider, within the bound.
No kernel may reach another device: no remote copies, remote signals or barrier semaphores. Data moves between devices by JAX's collectives and lax.ppermute only.
A program may use at most 64 MiB of HBM per device.

v0:
```python
import jax
import jax.numpy as jnp
from jax import lax
from jax.sharding import PartitionSpec as P

BLK = 128
TOP = 16384.0
TINY = 1.1754943508222875e-38
PAD = 16


def encode(piece):
    values = piece.astype(jnp.float32)
    largest = jnp.max(jnp.abs(values), axis=0, keepdims=True)
    exponent = jnp.floor(jnp.log2(jnp.maximum(largest, TINY)))
    coded = (values * jnp.exp2(-exponent) * TOP).astype(jnp.float16)
    header = jnp.broadcast_to(exponent, (PAD, piece.shape[1])).astype(jnp.float16)
    return jnp.concatenate([coded, header], axis=0)


def decode(coded, count):
    parts = coded.reshape(count, -1, coded.shape[1]).astype(jnp.float32)
    height = parts.shape[1] - PAD
    scale = jnp.exp2(parts[:, height : height + 1, :])
    values = (parts[:, :height, :] * (1.0 / TOP) * scale).astype(jnp.bfloat16)
    return values.reshape(count * height, coded.shape[1])


def local(density, keep_square, keep_cube):
    tile_rows, tile_cols = density.shape
    reps = lax.axis_size("rep")
    row_count = lax.axis_size("row")
    col_count = lax.axis_size("col")
    rep = lax.axis_index("rep")
    own = tile_rows // reps
    halves = tile_cols // tile_rows

    def section(array):
        cut = [
            lax.dynamic_slice_in_dim(array, half * tile_rows + rep * own, own, 0)
            for half in range(halves)
        ]
        return jnp.concatenate(cut, axis=0)

    right_piece = lax.dynamic_slice_in_dim(density, rep * own, own, 0)
    left_piece = section(density.T)
    left = decode(lax.all_gather(encode(left_piece), "col", axis=0, tiled=True), col_count)
    right = decode(lax.all_gather(encode(right_piece), "row", axis=0, tiled=True), row_count)

    def contract(a, b):
        return lax.dot_general(a, b, (((0,), (0,)), ((), ())), preferred_element_type=jnp.float32)

    partial = contract(right, left)
    partial = partial.reshape(halves, reps, own, tile_rows).transpose(1, 0, 2, 3)
    partial = partial.reshape(reps, halves * own, tile_rows)
    square_t = jnp.sum(lax.all_to_all(partial, "rep", 0, 0), axis=0)
    mask_rows = section(jnp.repeat(keep_square.T.astype(jnp.float32), BLK, axis=0))
    square_t = square_t * jnp.repeat(mask_rows, BLK, axis=1)
    low = decode(
        lax.all_gather(encode(square_t.astype(jnp.bfloat16)), "col", axis=0, tiled=True), col_count
    )
    cube = contract(low, right)
    mask = jnp.repeat(jnp.repeat(keep_cube.astype(jnp.float32), BLK, axis=0), BLK, axis=1)
    placed = jnp.zeros((tile_cols, tile_rows), jnp.float32)
    for half in range(halves):
        placed = lax.dynamic_update_slice_in_dim(
            placed, square_t[half * own : (half + 1) * own], half * tile_rows + rep * own, 0
        )
    total = 3.0 * placed.T - 2.0 * cube * mask
    pieces = lax.all_to_all(total.reshape(reps, own, tile_cols), "rep", 0, 0)
    return jnp.sum(pieces, axis=0)


def solution(mesh):
    return jax.shard_map(
        local,
        mesh=mesh,
        in_specs=(P("row", "col"), P("row", "col"), P("row", "col")),
        out_specs=P(("row", "rep"), "col"),
        check_vma=False,
    )
```

profile of v0, /device:TPU:1, one launch (start us, length us, event | category | flops | bytes accessed | tf_op | source)
XLA Modules:
  0.0 156.7 jit_solution(12126970050853005048)
XLA Ops:
  0.0 0.9 fusion.11
  1.0 1.0 fusion.13
  2.0 49.8 %all-gather.3 = f16[1792,768]{1,0:T(8,128)(2,1)S(1)} all-gather(f16[112,768]{1,0:T(8,128)(2,1)S(1)} %pad_maximum_fusion.3), channel_id=1, replica_groups=mesh['row'=16,'col'=8,'rep'=4] {'row'}, dimensions={0}, use_global_device_ids=true | all-gather | bytes 2924544 | tf_op jit(solution)/shard_map/all_gather | solution.py:48
  51.8 0.5 convert.3
  52.4 0.1 fusion.15
  52.5 0.5 fusion
  53.0 2.4 %copy.12 = bf16[1536,768]{0,1:T(8,128)(2,1)} copy(bf16[1536,768]{1,0:T(8,128)(2,1)S(1)} %bitcast.59) | data formatting | bytes 4718592 | tf_op jit(solution)/shard_map/reshape | solution.py:26
  55.5 1.1 dynamic-slice_bitcast_fusion.1
  56.6 0.2 fusion.5
  56.9 0.2 fusion.7
  57.1 0.1 broadcast_in_dim.35
  57.2 0.1 pad_maximum_fusion.1
  57.3 0.2 copy.13
  57.5 21.3 %all-gather.4 = f16[1664,384]{1,0:T(8,128)(2,1)S(1)} all-gather(f16[208,384]{1,0:T(8,128)(2,1)S(1)} %copy.13), channel_id=1, replica_groups=mesh['row'=16,'col'=8,'rep'=4] {'col'}, dimensions={0}, use_global_device_ids=true | all-gather | bytes 1437696 | tf_op jit(solution)/shard_map/all_gather | solution.py:47
  78.9 0.2 convert.4
  79.1 0.0 copy-start
  79.1 0.2 fusion.2
  79.3 1.4 copy-done
  80.7 1.4 convolution_bitcast_fusion
  82.1 1.1 copy.14
  83.3 4.4 %all-to-all-start = ((f32[4,192,384]{2,1,0:T(8,128)}), f32[4,192,384]{2,1,0:T(8,128)}, u32[]{:S(2)}, u32[]{:S(2)}) async-start(f32[4,192,384]{2,1,0:T(8,128)} %bitcast.13), calls=%async_computation | async-start | bytes 2359296 | tf_op jit(solution)/shard_map/all_to_all | solution.py:56
  87.7 0.0 copy-done.1
  87.7 0.1 broadcast_bitcast_fusion.1
  87.8 0.0 copy-done.2
  87.8 0.1 copy.17
  87.9 0.1 broadcast_bitcast_fusion
  87.9 1.1 broadcast_in_dim.40
  89.0 1.6 %copy.18 = f32[384,768]{1,0:T(8,128)S(1)} copy(f32[384,768]{0,1:T(8,128)} %bitcast.66) | data formatting | bytes 2359296 | tf_op jit(solution)/shard_map/reshape | solution.py:63
  90.7 0.1 constant_dynamic-slice_fusion.1
  90.8 0.1 pad_maximum_fusion.4
  90.8 13.1 %all-to-all-done = f32[4,192,384]{2,1,0:T(8,128)} async-done(((f32[4,192,384]{2,1,0:T(8,128)}), f32[4,192,384]{2,1,0:T(8,128)}, u32[]{:S(2)}, u32[]{:S(2)}) %all-to-all-start) | async-done | bytes 1179680 | tf_op jit(solution)/shard_map/all_to_all | solution.py:56
  103.9 2.1 %reduce_sum.18 = f32[192,384]{1,0:T(8,128)} reduce(f32[4,192,384]{2,1,0:T(8,128)} %all-to-all-done, f32[]{:T(128)} %constant.15.clone.1), dimensions={0}, to_apply=%region_2.0 | reduce | flops 221184 | bytes 1474564 | tf_op jit(solution)/shard_map/reduce_sum | solution.py:56
  106.0 1.9 %copy.15 = f32[192,384]{0,1:T(8,128)} copy(f32[192,384]{1,0:T(8,128)} %reduce_sum.18) | data formatting | bytes 589824 | tf_op jit(solution)/shard_map/reduce_sum | solution.py:56
  107.9 1.1 fusion.8
  109.0 0.8 fusion.23
  109.8 0.1 fusion.10
  110.0 0.1 broadcast_in_dim.38
  110.1 0.8 pad_maximum_fusion.2
  110.9 1.7 %copy.16 = f16[208,384]{1,0:T(8,128)(2,1)} copy(f16[208,384]{0,1:T(8,128)(2,1)} %pad_maximum_fusion.2) | data formatting | bytes 319488 | tf_op jit(solution)/shard_map/concatenate | solution.py:18
  112.6 15.4 %all-gather.5 = f16[1664,384]{1,0:T(8,128)(2,1)S(1)} all-gather(f16[208,384]{1,0:T(8,128)(2,1)} %copy.16), channel_id=1, replica_groups=mesh['row'=16,'col'=8,'rep'=4] {'col'}, dimensions={0}, use_global_device_ids=true | all-gather | bytes 1437696 | tf_op jit(solution)/shard_map/all_gather | solution.py:60
  128.0 0.2 convert.5
  128.2 1.2 fusion.1
  129.4 1.1 broadcast_in_dim.16
  130.6 2.0 %dynamic_update_slice.6 = f32[768,384]{0,1:T(8,128)} dynamic-update-slice(f32[768,384]{0,1:T(8,128)} %broadcast_in_dim.16, f32[96,384]{0,1:T(8,128)} %get-tuple-element.10, s32[]{:T(128)S(6)} %select_n.14, s32[]{:T(128)} %constant.18.clone.1) | dynamic-update-slice | bytes 294916 | tf_op jit(solution)/shard_map/dynamic_update_slice | solution.py:66
  132.5 1.9 %dynamic_update_slice.7 = f32[768,384]{0,1:T(8,128)} dynamic-update-slice(f32[768,384]{0,1:T(8,128)} %dynamic_update_slice.6, f32[96,384]{0,1:T(8,128)} %get-tuple-element.9, s32[]{:T(128)S(6)} %select_n.15, s32[]{:T(128)} %constant.18.clone.1) | dynamic-update-slice | bytes 294916 | tf_op jit(solution)/shard_map/dynamic_update_slice | solution.py:66
  134.5 2.8 %fusion.4 = f32[384,768]{1,0:T(8,128)S(1)} fusion(f32[384,768]{1,0:T(8,128)S(1)} %copy.18, bf16[1536,384]{1,0:T(8,128)(2,1)} %bitcast.65, bf16[1536,768]{1,0:T(8,128)(2,1)S(1)} %bitcast.60, f32[768,384]{0,1:T(8,128)} %dynamic_update_slice.7), kind=kOutput, calls=%fused_computation.9 | convolution fusion | flops 907149312 | bytes 7077888 | tf_op jit(solution)/shard_map/dot_general | solution.py:51
  137.3 18.7 %all_to_all.10 = f32[4,96,768]{2,1,0:T(8,128)S(1)} all-to-all(f32[4,96,768]{2,1,0:T(8,128)S(1)} %bitcast.64), channel_id=1, replica_groups=mesh['row'=16,'col'=8,'rep'=4] {'rep'}, dimensions={0} | all-to-all | bytes 2359296 | tf_op jit(solution)/shard_map/all_to_all | solution.py:70
  155.9 0.8 reduce_sum.19
  (16 shorter events, 0.2 us)
Async XLA Ops:
  79.1 1.7 %copy-start = (bf16[1536,768]{0,1:T(8,128)(2,1)S(1)}, bf16[1536,768]{0,1:T(8,128)(2,1)}, u32[]{:S(2)}) copy-start(bf16[1536,768]{0,1:T(8,128)(2,1)} %copy.12) | copy-start | bytes 7077892
  83.2 4.4 %copy-start.1 = (s32[3,6]{1,0:T(4,128)S(1)}, s32[3,6]{1,0:T(4,128)}, u32[]{:S(2)}) copy-start(s32[3,6]{1,0:T(4,128)} %param.4) | copy-start | bytes 220
  83.2 4.5 %copy-start.2 = (s32[3,6]{1,0:T(4,128)S(1)}, s32[3,6]{1,0:T(4,128)}, u32[]{:S(2)}) copy-start(s32[3,6]{1,0:T(4,128)} %param.5) | copy-start | bytes 220
  83.3 20.7 %all-to-all-start = ((f32[4,192,384]{2,1,0:T(8,128)}), f32[4,192,384]{2,1,0:T(8,128)}, u32[]{:S(2)}, u32[]{:S(2)}) async-start(f32[4,192,384]{2,1,0:T(8,128)} %bitcast.13), calls=%async_computation | async-start | bytes 2359296 | tf_op jit(solution)/shard_map/all_to_all | solution.py:56
where the time goes:
time: 157 us
  blocking collectives  105 us (67%)
  local copies, waits for them, and re-layouts  19.1 us (12%)
  waiting for transfers between devices  13.1 us (8%)
  other arithmetic  10.5 us (7%)
  starting transfers between devices  4.39 us (3%)
  matrix products  4.17 us (3%)
    all_gather x1, blocking collectives, local(): lax.all_gather(encode(right_piece), 'row', axis=0, tiled=True)  49.8 us
    all_gather x1, blocking collectives, local(): lax.all_gather(encode(left_piece), 'col', axis=0, tiled=True)  21.3 us
    all_to_all x1, blocking collectives, local(): pieces = lax.all_to_all(total.reshape(reps, own, tile_cols), 'rep', 0, 0)  18.7 us
    all_gather x1, blocking collectives, local(): lax.all_gather(encode(square_t.astype(jnp.bfloat16)), 'col', axis=0, tile...  15.4 us
    all_to_all x1, waiting for transfers between devices, local(): square_t = jnp.sum(lax.all_to_all(partial, 'rep', 0, 0), axis=0)  13.1 us
    all_to_all x1, starting transfers between devices, local(): square_t = jnp.sum(lax.all_to_all(partial, 'rep', 0, 0), axis=0)  4.39 us
    dot_general x2, matrix products, contract(): lax.dot_general(a, b, (((0,), (0,)), ((), ())), preferred_element_type=jn...  4.17 us
    dynamic_update_slice x2, local copies, waits for them, and re-layouts, local(): lax.dynamic_update_slice_in_dim(placed, square_t[half * own:(half + 1) *...  3.9 us
  transfers between devices with their start and end apart: 1, of which 1 were waited for; matrix products, arithmetic and copies ran while one was open for 2% of the time, Pallas kernels for 0%

commit v1 on v0

--- a/solution.py
+++ b/solution.py
@@ -7,6 +7,11 @@
 TOP = 16384.0
 TINY = 1.1754943508222875e-38
 PAD = 16
+
+
+def gather_by_exchange(value, axis, dim):
+    copies = jnp.concatenate([value] * lax.axis_size(axis), axis=dim)
+    return lax.all_to_all(copies, axis, dim, dim, tiled=True)
 
 
 def encode(piece):
@@ -44,7 +49,7 @@
 
     right_piece = lax.dynamic_slice_in_dim(density, rep * own, own, 0)
     left_piece = section(density.T)
-    left = decode(lax.all_gather(encode(left_piece), "col", axis=0, tiled=True), col_count)
+    left = decode(gather_by_exchange(encode(left_piece), "col", 0), col_count)
     right = decode(lax.all_gather(encode(right_piece), "row", axis=0, tiled=True), row_count)
 
     def contract(a, b):

time: 157 us -> 146 us (0.930)
  blocking collectives: 105 us -> 85.8 us
  starting transfers between devices: 4.39 us -> 15.5 us
  waiting for transfers between devices: 13.1 us -> 7.3 us
  local copies, waits for them, and re-layouts: 19.1 us -> 22.8 us
    all_gather x1 -> x0, blocking collectives: 21.3 us -> none  [local(): lax.all_gather(encode(left_piece), 'col', axis=0, tiled=True)]
    all_to_all x0 -> x1, starting transfers between devices: none -> 11.1 us  [gather_by_exchange(): return lax.all_to_all(copies, axis, dim, dim, tiled=True)]
    all_gather x1, blocking collectives: 15.4 us -> 22.5 us  [local(): lax.all_gather(encode(square_t.astype(jnp.bfloat16)), 'col', axis=0, tile...]
    all_to_all x1, waiting for transfers between devices: 13.1 us -> 7.3 us  [local(): square_t = jnp.sum(lax.all_to_all(partial, 'rep', 0, 0), axis=0)]
    all_gather x1, blocking collectives: 49.8 us -> 44.7 us  [local(): lax.all_gather(encode(right_piece), 'row', axis=0, tiled=True)]
    concatenate x0 -> x2, local copies, waits for them, and re-layouts: none -> 3.84 us  [gather_by_exchange(): copies = jnp.concatenate([value] * lax.axis_size(axis), axis=dim)]
  transfers between devices with their start and end apart: 1 -> 2, of which waited for: 1 -> 1; matrix products, arithmetic and copies ran while one was open for 2% -> 5% of each run, Pallas kernels for 0% -> 0%
where the time goes in v1:
time: 146 us
  blocking collectives  85.8 us (59%)
  local copies, waits for them, and re-layouts  22.8 us (16%)
  starting transfers between devices  15.5 us (11%)
  other arithmetic  9.92 us (7%)
  waiting for transfers between devices  7.3 us (5%)
  matrix products  4.18 us (3%)
    all_gather x1, blocking collectives, local(): lax.all_gather(encode(right_piece), 'row', axis=0, tiled=True)  44.7 us
    all_gather x1, blocking collectives, local(): lax.all_gather(encode(square_t.astype(jnp.bfloat16)), 'col', axis=0, tile...  22.5 us
    all_to_all x1, blocking collectives, local(): pieces = lax.all_to_all(total.reshape(reps, own, tile_cols), 'rep', 0, 0)  18.6 us
    all_to_all x1, starting transfers between devices, gather_by_exchange(): return lax.all_to_all(copies, axis, dim, dim, tiled=True)  11.1 us
    all_to_all x1, waiting for transfers between devices, local(): square_t = jnp.sum(lax.all_to_all(partial, 'rep', 0, 0), axis=0)  7.3 us
    all_to_all x1, starting transfers between devices, local(): square_t = jnp.sum(lax.all_to_all(partial, 'rep', 0, 0), axis=0)  4.39 us
    dot_general x2, matrix products, contract(): lax.dot_general(a, b, (((0,), (0,)), ((), ())), preferred_element_type=jn...  4.18 us
    dynamic_update_slice x2, local copies, waits for them, and re-layouts, local(): lax.dynamic_update_slice_in_dim(placed, square_t[half * own:(half + 1) *...  3.92 us
  transfers between devices with their start and end apart: 2, of which 1 were waited for; matrix products, arithmetic and copies ran while one was open for 5% of the time, Pallas kernels for 0%

profile of v1, /device:TPU:1, one launch (start us, length us, event | category | flops | bytes accessed | tf_op | source)
XLA Modules:
  0.0 145.7 jit_solution(1225307709783766593)
XLA Ops:
  0.0 1.1 dynamic-slice_bitcast_fusion.1
  1.1 0.2 fusion.5
  1.4 0.2 fusion.7
  1.6 0.1 broadcast_in_dim.35
  1.7 1.9 %concatenate.19 = f16[1664,384]{0,1:T(8,128)(2,1)S(1)} concatenate(f16[192,384]{0,1:T(8,128)(2,1)S(1)} %fusion.7, f16[16,384]{0,1:T(8,128)(2,1)S(1)} %broadcast_in_dim.35, f16[192,384]{0,1:T(8,128)(2,1)S(1)} %fusion.7, f16[16,384]{0,1:T(8,128)(2,1)S(1)} %broadcast_in_dim.35, f16[192,384]{0,1:T(8,128)(2,1)S(1)} %fusion.7, f16[16,384]{0,1:T(8,128)(2,1)S(1)} %broadcast_in_dim.35, ...), dimensions={0} | concatenate | bytes 2555904 | tf_op jit(solution)/shard_map/concatenate | solution.py:13
  3.7 1.9 %copy.13 = f16[1664,384]{1,0:T(8,128)(2,1)} copy(f16[1664,384]{0,1:T(8,128)(2,1)S(1)} %concatenate.19) | data formatting | bytes 2555904 | tf_op jit(solution)/shard_map/concatenate | solution.py:13
  5.6 11.1 %all-to-all-start = ((f16[8,208,384]{2,1,0:T(8,128)(2,1)}), f16[8,208,384]{2,1,0:T(8,128)(2,1)}, u32[]{:S(2)}, u32[]{:S(2)}) async-start(f16[8,208,384]{2,1,0:T(8,128)(2,1)} %bitcast.7), calls=%async_computation | async-start | bytes 2555904 | tf_op jit(solution)/shard_map/all_to_all | solution.py:14
  16.7 0.0 copy-done.1
  16.8 0.1 fusion.13
  16.9 44.7 %all-gather.2 = f16[1792,768]{1,0:T(8,128)(2,1)S(1)} all-gather(f16[112,768]{1,0:T(8,128)(2,1)S(1)} %pad_maximum_fusion.2), channel_id=1, replica_groups=mesh['row'=16,'col'=8,'rep'=4] {'row'}, dimensions={0}, use_global_device_ids=true | all-gather | bytes 2924544 | tf_op jit(solution)/shard_map/all_gather | solution.py:53
  61.6 0.5 convert.2
  62.1 0.1 fusion.15
  62.2 0.5 fusion
  62.7 2.5 %copy.12 = bf16[1536,768]{0,1:T(8,128)(2,1)} copy(bf16[1536,768]{1,0:T(8,128)(2,1)S(1)} %bitcast.58) | data formatting | bytes 4718592 | tf_op jit(solution)/shard_map/reshape | solution.py:31
  65.2 0.0 all-to-all-done
  65.2 1.5 %convert_element_type.83 = f32[8,208,384]{2,1,0:T(8,128)S(1)} convert(f16[8,208,384]{2,1,0:T(8,128)(2,1)} %all-to-all-done) | non-fusion elementwise | flops 638976 | bytes 3833856 | tf_op jit(solution)/shard_map/convert_element_type | solution.py:27
  66.7 0.0 copy-start
  66.7 0.2 fusion.2
  67.0 1.4 copy-done
  68.4 1.4 convolution_bitcast_fusion
  69.8 1.1 copy.14
  70.9 4.4 %all-to-all-start.1 = ((f32[4,192,384]{2,1,0:T(8,128)}), f32[4,192,384]{2,1,0:T(8,128)}, u32[]{:S(2)}, u32[]{:S(2)}) async-start(f32[4,192,384]{2,1,0:T(8,128)} %bitcast.12), calls=%async_computation.1 | async-start | bytes 2359296 | tf_op jit(solution)/shard_map/all_to_all | solution.py:61
  75.3 0.0 copy-done.2
  75.3 0.1 broadcast_bitcast_fusion.1
  75.4 0.1 copy.17
  75.5 0.1 broadcast_bitcast_fusion
  75.6 1.1 broadcast_in_dim.40
  76.7 1.6 %copy.18 = f32[384,768]{1,0:T(8,128)S(1)} copy(f32[384,768]{0,1:T(8,128)} %bitcast.64) | data formatting | bytes 2359296 | tf_op jit(solution)/shard_map/reshape | solution.py:68
  78.3 0.1 constant_dynamic-slice_fusion.1
  78.4 0.1 pad_maximum_fusion.3
  78.5 7.3 %all-to-all-done.1 = f32[4,192,384]{2,1,0:T(8,128)} async-done(((f32[4,192,384]{2,1,0:T(8,128)}), f32[4,192,384]{2,1,0:T(8,128)}, u32[]{:S(2)}, u32[]{:S(2)}) %all-to-all-start.1) | async-done | bytes 1179680 | tf_op jit(solution)/shard_map/all_to_all | solution.py:61
  85.8 2.1 %reduce_sum.18 = f32[192,384]{1,0:T(8,128)} reduce(f32[4,192,384]{2,1,0:T(8,128)} %all-to-all-done.1, f32[]{:T(128)} %constant.15.clone.1), dimensions={0}, to_apply=%region_2.0 | reduce | flops 221184 | bytes 1474564 | tf_op jit(solution)/shard_map/reduce_sum | solution.py:61
  87.9 1.9 %copy.15 = f32[192,384]{0,1:T(8,128)} copy(f32[192,384]{1,0:T(8,128)} %reduce_sum.18) | data formatting | bytes 589824 | tf_op jit(solution)/shard_map/reduce_sum | solution.py:61
  89.8 1.1 fusion.8
  90.9 0.8 fusion.23
  91.7 0.1 fusion.10
  91.9 0.1 broadcast_in_dim.38
  92.0 0.8 pad_maximum_fusion.1
  92.8 1.7 %copy.16 = f16[208,384]{1,0:T(8,128)(2,1)} copy(f16[208,384]{0,1:T(8,128)(2,1)} %pad_maximum_fusion.1) | data formatting | bytes 319488 | tf_op jit(solution)/shard_map/concatenate | solution.py:23
  94.5 22.5 %all-gather.3 = f16[1664,384]{1,0:T(8,128)(2,1)S(1)} all-gather(f16[208,384]{1,0:T(8,128)(2,1)} %copy.16), channel_id=1, replica_groups=mesh['row'=16,'col'=8,'rep'=4] {'col'}, dimensions={0}, use_global_device_ids=true | all-gather | bytes 1437696 | tf_op jit(solution)/shard_map/all_gather | solution.py:65
  117.0 0.2 convert.3
  117.2 1.2 fusion.1
  118.4 1.1 broadcast_in_dim.16
  119.6 2.0 %dynamic_update_slice.6 = f32[768,384]{0,1:T(8,128)} dynamic-update-slice(f32[768,384]{0,1:T(8,128)} %broadcast_in_dim.16, f32[96,384]{0,1:T(8,128)} %get-tuple-element.10, s32[]{:T(128)S(6)} %select_n.14, s32[]{:T(128)} %constant.18.clone.1) | dynamic-update-slice | bytes 294916 | tf_op jit(solution)/shard_map/dynamic_update_slice | solution.py:71
  121.5 2.0 %dynamic_update_slice.7 = f32[768,384]{0,1:T(8,128)} dynamic-update-slice(f32[768,384]{0,1:T(8,128)} %dynamic_update_slice.6, f32[96,384]{0,1:T(8,128)} %get-tuple-element.9, s32[]{:T(128)S(6)} %select_n.15, s32[]{:T(128)} %constant.18.clone.1) | dynamic-update-slice | bytes 294916 | tf_op jit(solution)/shard_map/dynamic_update_slice | solution.py:71
  123.5 2.8 %fusion.4 = f32[384,768]{1,0:T(8,128)S(1)} fusion(f32[384,768]{1,0:T(8,128)S(1)} %copy.18, bf16[1536,384]{1,0:T(8,128)(2,1)} %bitcast.63, bf16[1536,768]{1,0:T(8,128)(2,1)S(1)} %bitcast.59, f32[768,384]{0,1:T(8,128)} %dynamic_update_slice.7), kind=kOutput, calls=%fused_computation.9 | convolution fusion | flops 907149312 | bytes 7077888 | tf_op jit(solution)/shard_map/dot_general | solution.py:56
  126.3 18.6 %all_to_all.19 = f32[4,96,768]{2,1,0:T(8,128)S(1)} all-to-all(f32[4,96,768]{2,1,0:T(8,128)S(1)} %bitcast.62), channel_id=1, replica_groups=mesh['row'=16,'col'=8,'rep'=4] {'rep'}, dimensions={0} | all-to-all | bytes 2359296 | tf_op jit(solution)/shard_map/all_to_all | solution.py:75
  144.9 0.8 reduce_sum.19
  (19 shorter events, 0.2 us)
Async XLA Ops:
  5.6 11.2 %copy-start.1 = (bf16[384,768]{1,0:T(8,128)(2,1)S(1)}, bf16[384,768]{1,0:T(8,128)(2,1)}, u32[]{:S(2)}) copy-start(bf16[384,768]{1,0:T(8,128)(2,1)} %param.3) | copy-start | bytes 1769476
  5.6 59.7 %all-to-all-start = ((f16[8,208,384]{2,1,0:T(8,128)(2,1)}), f16[8,208,384]{2,1,0:T(8,128)(2,1)}, u32[]{:S(2)}, u32[]{:S(2)}) async-start(f16[8,208,384]{2,1,0:T(8,128)(2,1)} %bitcast.7), calls=%async_computation | async-start | bytes 2555904 | tf_op jit(solution)/shard_map/all_to_all | solution.py:14
  66.7 1.7 %copy-start = (bf16[1536,768]{0,1:T(8,128)(2,1)S(1)}, bf16[1536,768]{0,1:T(8,128)(2,1)}, u32[]{:S(2)}) copy-start(bf16[1536,768]{0,1:T(8,128)(2,1)} %copy.12) | copy-start | bytes 7077892
  70.9 4.4 %copy-start.2 = (s32[3,6]{1,0:T(4,128)S(1)}, s32[3,6]{1,0:T(4,128)}, u32[]{:S(2)}) copy-start(s32[3,6]{1,0:T(4,128)} %param.4) | copy-start | bytes 220
  70.9 4.5 %copy-start.3 = (s32[3,6]{1,0:T(4,128)S(1)}, s32[3,6]{1,0:T(4,128)}, u32[]{:S(2)}) copy-start(s32[3,6]{1,0:T(4,128)} %param.5) | copy-start | bytes 220
  70.9 14.9 %all-to-all-start.1 = ((f32[4,192,384]{2,1,0:T(8,128)}), f32[4,192,384]{2,1,0:T(8,128)}, u32[]{:S(2)}, u32[]{:S(2)}) async-start(f32[4,192,384]{2,1,0:T(8,128)} %bitcast.12), calls=%async_computation.1 | async-start | bytes 2359296 | tf_op jit(solution)/shard_map/all_to_all | solution.py:61
